TPU v7x, 32 devices: a whole 2x2x4 slice. The times are simulated.
32 devices in a mesh: groups: 2 (over y), expert: 4 (over z), cuts: 4 (over x, core).
Axes of the slice: x: 2, y: 2, z: 4, core: 2. Of those that a mesh axis runs over, the one named last changes fastest.
Arguments:
- queries: bfloat16 [256, 6144], P(('groups', 'expert'), 'cuts'), parts along dimension 0, may hold values from -108 to 108
- key_cache: bfloat16 [256, 96, 1024], P(('groups', 'expert'), None, 'cuts'), parts along dimension 0, may hold values from -4.5 to 4.5
- value_cache: bfloat16 [256, 96, 1024], P(('groups', 'expert'), None, 'cuts'), parts along dimension 0, may hold values from -6 to 6
- lengths: int32 [256], P(('groups', 'expert')), parts along dimension 0, may hold values from 1 to 96, as said below
- residual: bfloat16 [256, 6144], P(('groups', 'expert'), 'cuts'), parts along dimension 0, may hold values from -6 to 6
- routes: int32 [256, 4], P(('groups', 'expert')), parts along dimension 0, may hold values from 0 to 15, all different within a row; in each aligned block of 32 rows (0 to 31, 32 to 63, ...) at most 8 rows name the same one
- route_weight: float32 [256, 4], P(('groups', 'expert')), parts along dimension 0, may hold values from 0.2 to 1
- gate_weight: bfloat16 [4, 6144, 4096], P('expert', None, 'cuts'), may hold values from -0.078125 to 0.078125
- up_weight: bfloat16 [4, 6144, 4096], P('expert', None, 'cuts'), may hold values from -0.078125 to 0.078125
- down_weight: bfloat16 [4, 4096, 6144], P('expert', 'cuts'), may hold values from -0.0625 to 0.0625
Outputs:
- layer_out: bfloat16 [256, 6144], P(('groups', 'expert'), 'cuts'), parts along dimension 0
There are 2 independent parts, one for each index of `groups`. A program takes and returns all parts, laid end to end along the dimension named above; an argument that names none is the same for every part. Nothing has to cross between parts.
Inputs may be any that keep to these rules, and one draw needn't show every extreme that they name: `lengths`: the first row of each device's block of 32 rows has length 96. `routes`: each row names 4 different experts; within each device's block of 32 rows no expert is named by more than 8 rows.
All inputs are finite; a program needn't handle non-finite values.
Results may differ from a plain program's by a relative error of at most 0.007.
Values may be sent and summed in bfloat16 or wider, within the bound.
A program may use at most 128 MiB of HBM per device.

v0:
```python
import math

import jax
import jax.numpy as jnp
from jax import lax
from jax.sharding import PartitionSpec as P

HEADS = 48
KV_HEADS = 8
HEAD = 128
MODEL_EXPERTS = 16
TOPK = 4
EXPERTS = 2


def on_device(
    queries,
    key_cache,
    value_cache,
    lengths,
    residual,
    routes,
    route_weight,
    gate_weight,
    up_weight,
    down_weight,
):
    row_count = queries.shape[0]
    context = key_cache.shape[1]
    kv_local = key_cache.shape[2] // HEAD
    group_size = HEADS // KV_HEADS
    query_heads = queries.reshape(row_count, kv_local, group_size, HEAD)
    key_heads = key_cache.reshape(row_count, context, kv_local, HEAD)
    scores = jnp.einsum(
        "rkgj,rtkj->rkgt", query_heads, key_heads, preferred_element_type=jnp.float32
    ) / math.sqrt(HEAD)
    visible = (
        jnp.arange(context, dtype=jnp.int32)[None, None, None, :] < lengths[:, None, None, None]
    )
    scores = jnp.where(visible, scores, -jnp.inf)
    highest = jnp.max(scores, axis=-1, keepdims=True)
    scaled = jnp.exp(scores - highest)
    probabilities = (scaled / jnp.sum(scaled, axis=-1, keepdims=True)).astype(jnp.bfloat16)
    value_heads = value_cache.reshape(row_count, context, kv_local, HEAD)
    attended = jnp.einsum(
        "rkgt,rtkj->rkgj", probabilities, value_heads, preferred_element_type=jnp.float32
    )
    hidden = residual.astype(jnp.float32) + attended.reshape(row_count, -1)
    inputs = hidden.astype(jnp.bfloat16)
    devices = lax.axis_size("expert")
    expert_count = EXPERTS
    splits = devices // expert_count
    capacity = (row_count * TOPK + MODEL_EXPERTS - 1) // MODEL_EXPERTS
    expert_ids = jnp.arange(expert_count, dtype=jnp.int32)
    onehot = (routes[:, :, None] == expert_ids[None, None, :]).astype(jnp.float32)
    routed = jnp.sum(onehot, axis=1)
    gate_share = jnp.sum(onehot * route_weight[:, :, None], axis=1)
    earlier = jnp.cumsum(routed, axis=0) - routed
    slot_index = jnp.arange(capacity, dtype=jnp.float32)
    chosen = routed.T[:, None, :] * (earlier.T[:, None, :] == slot_index[None, :, None]).astype(
        jnp.float32
    )
    weighted = jnp.repeat(chosen * gate_share.T[:, None, :], splits, axis=0)
    chosen_rows = chosen.astype(jnp.bfloat16)
    outgoing = jnp.einsum(
        "ecr,rf->ecf", chosen_rows, inputs, preferred_element_type=jnp.float32
    ).astype(jnp.bfloat16)
    outgoing = jnp.repeat(outgoing, splits, axis=0)
    arrived = lax.all_gather(
        lax.all_to_all(outgoing, "expert", split_axis=0, concat_axis=0, tiled=True),
        "cuts",
        axis=2,
        tiled=True,
    )
    senders = arrived.shape[0]
    item_count = arrived.shape[1]
    stacked = arrived.reshape(senders * item_count, arrived.shape[2])
    gate_act = jnp.dot(stacked, gate_weight[0], preferred_element_type=jnp.float32)
    up_act = jnp.dot(stacked, up_weight[0], preferred_element_type=jnp.float32)
    activated = (jax.nn.silu(gate_act) * up_act).astype(jnp.bfloat16)
    partial_out = jnp.dot(activated, down_weight[0], preferred_element_type=jnp.float32)
    partial_out = partial_out.reshape(senders, item_count, partial_out.shape[1])
    returned = lax.all_to_all(partial_out, "expert", split_axis=0, concat_axis=0, tiled=True)
    full_rows = jnp.einsum("ncr,ncf->rf", weighted, returned, precision=lax.Precision.HIGHEST)
    combined = lax.psum_scatter(
        full_rows.astype(jnp.bfloat16), "cuts", scatter_dimension=1, tiled=True
    ).astype(jnp.float32)
    return (hidden + combined).astype(jnp.bfloat16)


def solution(mesh):
    return jax.shard_map(
        on_device,
        mesh=mesh,
        in_specs=(
            P(("groups", "expert"), "cuts"),
            P(("groups", "expert"), None, "cuts"),
            P(("groups", "expert"), None, "cuts"),
            P(("groups", "expert")),
            P(("groups", "expert"), "cuts"),
            P(("groups", "expert"), None),
            P(("groups", "expert"), None),
            P("expert", None, "cuts"),
            P("expert", None, "cuts"),
            P("expert", "cuts", None),
        ),
        out_specs=P(("groups", "expert"), "cuts"),
        check_vma=False,
    )
```

profile of v0, /device:TPU:0, one launch (start us, length us, event | category | flops | bytes accessed | tf_op | source)
XLA Modules:
  0.0 106.0 jit_solution(14646942957490622218)
XLA Ops:
  6.5 0.8 convert_reduce_fusion
  7.4 0.1 copy.25
  7.5 0.1 reduce_window_sum.13
  7.5 0.1 copy.27
  7.6 0.1 copy.28
  7.7 1.0 reshape.51
  8.7 0.7 iota_compare_fusion
  9.4 2.3 %fusion.18 = f32[32,2,6,96]{3,2,1,0:T(8,128)S(1)} fusion(bf16[32,2,6,128]{3,2,1,0:T(8,128)(2,1)S(1)} %reshape.51, pred[32,96]{1,0:T(8,128)(4,1)S(1)} %iota_compare_fusion, bf16[32,96,256]{2,1,0:T(8,128)(2,1)} %param.11), kind=kOutput, calls=%fused_computation.18 | convolution fusion | flops 9510912 | bytes 1821696 | tf_op jit(solution)/shard_map/rkgj,rtkj->rkgt/dot_general | solution.py:34
  11.8 0.3 fusion.51
  12.1 0.0 copy-start.1
  12.1 0.9 fusion.8
  13.0 0.1 reshape.54
  13.1 0.1 convolution_convert_fusion
  13.2 12.0 %all_to_all.10 = bf16[4,8,1536]{2,1,0:T(8,128)(2,1)S(1)} all-to-all(bf16[4,8,1536]{2,1,0:T(8,128)(2,1)S(1)} %bitcast.65), channel_id=1, replica_groups=mesh['groups'=2,'expert'=4,'cuts'=4] {'expert'}, dimensions={0} | all-to-all | bytes 196608 | tf_op jit(solution)/shard_map/all_to_all | solution.py:70
  25.2 6.4 %all_gather.3 = bf16[4,8,6144]{2,1,0:T(8,128)(2,1)S(1)} all-gather(bf16[4,8,1536]{2,1,0:T(8,128)(2,1)S(1)} %all_to_all.10), channel_id=1, replica_groups=mesh['groups'=2,'expert'=4,'cuts'=4] {'cuts'}, dimensions={2}, use_global_device_ids=true | all-gather | bytes 491520 | tf_op jit(solution)/shard_map/all_gather | solution.py:69
  31.6 6.8 %fusion.5 = f32[32,1024]{1,0:T(8,128)S(1)} fusion(bf16[1,6144,1024]{2,1,0:T(8,128)(2,1)} %param.17, bf16[4,8,6144]{2,1,0:T(8,128)(2,1)S(1)} %all_gather.3), kind=kOutput, calls=%fused_computation.5 | convolution fusion | flops 402653184 | bytes 13107200 | tf_op jit(solution)/shard_map/dot_general | solution.py:78
  38.5 13.4 %fusion.1 = f32[4,8,6144]{2,1,0:T(8,128)} fusion(bf16[1,1024,6144]{2,1,0:T(8,128)(2,1)} %param.19, bf16[1,6144,1024]{2,1,0:T(8,128)(2,1)} %param.18, bf16[4,8,6144]{2,1,0:T(8,128)(2,1)S(1)} %all_gather.3, f32[32,1024]{1,0:T(8,128)S(1)} %fusion.5), kind=kOutput, calls=%fused_computation.1 | convolution fusion | flops 805502976 | bytes 26476544 | tf_op jit(solution)/shard_map/dot_general | solution.py:81
  51.9 3.5 %all-to-all-start.1 = ((f32[4,8,6144]{2,1,0:T(8,128)}), f32[4,8,6144]{2,1,0:T(8,128)S(1)}, u32[]{:S(2)}, u32[]{:S(2)}) async-start(f32[4,8,6144]{2,1,0:T(8,128)} %fusion.1), calls=%async_computation.1 | async-start | bytes 1572864 | tf_op jit(solution)/shard_map/all_to_all | solution.py:83
  55.4 0.0 reduce-scatter.2.cloned.1.call-start
  55.4 20.8 %all-to-all-done.1 = f32[4,8,6144]{2,1,0:T(8,128)S(1)} async-done(((f32[4,8,6144]{2,1,0:T(8,128)}), f32[4,8,6144]{2,1,0:T(8,128)S(1)}, u32[]{:S(2)}, u32[]{:S(2)}) %all-to-all-start.1) | async-done | bytes 786464 | tf_op jit(solution)/shard_map/all_to_all | solution.py:83
  76.2 1.6 %fusion.7 = bf16[32,6144]{1,0:T(8,128)(2,1)} fusion(f32[4,8,32]{2,1,0:T(8,128)S(1)} %bitcast.67, f32[4,8,6144]{2,1,0:T(8,128)S(1)} %all-to-all-done.1), kind=kOutput, calls=%fused_computation.8 | convolution fusion | flops 75694080 | bytes 1183744 | tf_op jit(solution)/shard_map/ncr,ncf->rf/dot_general | solution.py:84
  77.8 0.0 reduce-scatter.2.cloned.1.call-update
  77.8 19.8 %reduce-scatter.2.cloned.1.call-done = bf16[32,1536]{1,0:T(8,128)(2,1)} async-done(((bf16[32,6144]{1,0:T(8,128)(2,1)}), bf16[32,1536]{1,0:T(8,128)(2,1)}) %reduce-scatter.2.cloned.1.call-update) | async-done | bytes 98320 | tf_op jit(solution)/shard_map/reduce_scatter | solution.py:85
  97.6 1.6 %add_convert_fusion = bf16[32,1536]{1,0:T(8,128)(2,1)} fusion(bf16[32,1536]{1,0:T(8,128)(2,1)} %reduce-scatter.2.cloned.1.call-done, f32[32,1536]{1,0:T(8,128)S(1)} %reshape.54, bf16[32,1536]{1,0:T(8,128)(2,1)S(1)} %copy-done.1), kind=kLoop, calls=%fused_computation.26 | loop fusion | flops 245760 | bytes 491520 | tf_op jit(solution)/shard_map/convert_element_type | solution.py:88
  (7 shorter events, 0.0 us)
Async XLA Ops:
  6.5 5.5 %copy-start = (bf16[32,96,256]{2,1,0:T(8,128)(2,1)S(1)}, bf16[32,96,256]{2,1,0:T(8,128)(2,1)}, u32[]{:S(2)}) copy-start(bf16[32,96,256]{2,1,0:T(8,128)(2,1)} %param.12) | copy-start | bytes 4718596
  12.1 1.0 copy-start.1
  51.9 24.4 %all-to-all-start.1 = ((f32[4,8,6144]{2,1,0:T(8,128)}), f32[4,8,6144]{2,1,0:T(8,128)S(1)}, u32[]{:S(2)}, u32[]{:S(2)}) async-start(f32[4,8,6144]{2,1,0:T(8,128)} %fusion.1), calls=%async_computation.1 | async-start | bytes 1572864 | tf_op jit(solution)/shard_map/all_to_all | solution.py:83
  55.4 42.2 %reduce-scatter.2.cloned.1.call-start = ((), (), s32[]{:S(2)}) async-start(), calls=%async_computation.3 | async-start | bytes 491520 | tf_op jit(solution)/shard_map/reduce_scatter | solution.py:85
Sparse Core Ops, SparseCore 0:
  77.9 19.6 reduce-scatter.1
where the time goes:
time: 106 us
  waiting for transfers between devices  40.6 us (38%)
  matrix products  25.2 us (24%)
  blocking collectives  18.4 us (17%)
  between operations  13.5 us (13%)
  starting transfers between devices  3.53 us (3%)
  other arithmetic  3.48 us (3%)
  local copies, waits for them, and re-layouts  1.35 us (1%)
    all_to_all x1, waiting for transfers between devices, on_device(): lax.all_to_all(partial_out, 'expert', split_axis=0, concat_axis=0, tiled=...  20.8 us
    reduce_scatter x1, waiting for transfers between devices, on_device(): lax.psum_scatter(full_rows.astype(jnp.bfloat16), 'cuts', scatter_dimensio...  19.8 us
    dot_general x1, matrix products, on_device(): jnp.dot(activated, down_weight[0], preferred_element_type=jnp.float32)  13.4 us
    all_to_all x1, blocking collectives, on_device(): lax.all_to_all(outgoing, 'expert', split_axis=0, concat_axis=0, tiled=True)  12 us
    dot_general x1, matrix products, on_device(): jnp.dot(stacked, gate_weight[0], preferred_element_type=jnp.float32)  6.83 us
    all_gather x1, blocking collectives, on_device(): lax.all_gather(lax.all_to_all(outgoing, 'expert', split_axis=0, concat_ax...  6.44 us
    all_to_all x1, starting transfers between devices, on_device(): lax.all_to_all(partial_out, 'expert', split_axis=0, concat_axis=0, tiled=...  3.49 us
    dot_general x1, matrix products, on_device(): jnp.einsum('rkgj,rtkj->rkgt', query_heads, key_heads, preferred_element_t...  2.31 us
  transfers between devices with their start and end apart: 2, of which 2 were waited for; matrix products, arithmetic and copies ran while one was open for 0% of the time, Pallas kernels for 0%

commit v1 on v0

v1 whole, which is shorter than its diff:
```python
import functools
import math

import jax
import jax.numpy as jnp
from jax import lax
from jax.experimental import pallas as pl
from jax.experimental.pallas import tpu as pltpu
from jax.sharding import PartitionSpec as P

HEADS = 48
KV_HEADS = 8
HEAD = 128
MODEL_EXPERTS = 16
TOPK = 4
EXPERTS = 2
SLOTS = 8
MESH = pl.DeviceIdType.MESH


def each(low, high, body):
    if high - low <= 8:
        for i in range(low, high):
            body(i)
    else:

        def step(i, carry):
            body(i)
            return carry

        lax.fori_loop(low, high, step, 0)


def cut_order(c, cuts):
    if cuts == 4:
        beside = c + 1 - 2 * lax.rem(c, 2)
        return [c, beside, lax.rem(c + 2, 4), lax.rem(beside + 2, 4)]
    return [lax.rem(c + i, cuts) for i in range(cuts)]


def kernel(
    devices,
    cuts,
    cap,
    lengths,
    routes,
    route_weight,
    queries,
    keys,
    values,
    residual,
    gate,
    up,
    down,
    out,
    q_buf,
    k_buf,
    v_buf,
    res_buf,
    q_rows,
    att_rows,
    hidden,
    wg,
    wu,
    wd,
    outgoing,
    arrived,
    stacked,
    gate_act,
    up_act,
    act,
    cut_send,
    cut_recv,
    own,
    back_send,
    back_recv,
    in_sem,
    wg_sem,
    wu_sem,
    wd_sem,
    row_send,
    row_recv,
    share_send,
    share_recv,
    sum_send,
    sum_recv,
    ret_send,
    ret_recv,
):
    b = lax.axis_index("expert")
    c = lax.axis_index("cuts")
    order = cut_order(c, cuts)
    row_count, width = q_buf.shape
    context = k_buf.shape[1]
    kv_local = k_buf.shape[2] // HEAD
    group = HEADS // KV_HEADS
    stride = kv_local * SLOTS
    splits = devices // EXPERTS
    half = width // 2
    ff = wg.shape[2]

    barrier = pltpu.get_barrier_semaphore()

    def greet(i):
        pl.semaphore_signal(
            barrier, inc=1, device_id={"expert": lax.rem(b + i, devices)}, device_id_type=MESH
        )

    each(1, devices, greet)
    for peer in order[1:]:
        pl.semaphore_signal(barrier, inc=1, device_id={"cuts": peer}, device_id_type=MESH)

    loads = [
        pltpu.make_async_copy(queries, q_buf, in_sem.at[0]),
        pltpu.make_async_copy(keys, k_buf, in_sem.at[1]),
        pltpu.make_async_copy(values, v_buf, in_sem.at[2]),
        pltpu.make_async_copy(residual, res_buf, in_sem.at[3]),
    ]
    gate_loads, up_loads, down_loads = [], [], []
    for i in range(cuts):
        rows = pl.ds(pl.multiple_of(order[i] * width, width), width)
        gate_loads.append(pltpu.make_async_copy(gate.at[0, rows, :], wg.at[i], wg_sem.at[i]))
        up_loads.append(pltpu.make_async_copy(up.at[0, rows, :], wu.at[i], wu_sem.at[i]))
    for i in range(cuts):
        columns = pl.ds(pl.multiple_of(order[cuts - 1 - i] * width, width), width)
        down_loads.append(pltpu.make_async_copy(down.at[0, :, columns], wd.at[i], wd_sem.at[i]))
    for load in loads:
        load.start()
    for g, u in zip(gate_loads, up_loads):
        g.start()
        u.start()
    for d in down_loads:
        d.start()

    slot = lax.broadcasted_iota(jnp.int32, (EXPERTS * cap, row_count), 0)
    expert_of = slot // cap
    routed = jnp.zeros((EXPERTS * cap, row_count), jnp.float32)
    share = jnp.zeros((EXPERTS * cap, row_count), jnp.float32)
    for k in range(TOPK):
        named = routes[k : k + 1, :] == expert_of
        routed = routed + jnp.where(named, 1.0, 0.0)
        share = share + jnp.where(named, route_weight[k : k + 1, :], 0.0)
    before = jnp.where(
        lax.broadcasted_iota(jnp.int32, (row_count, row_count), 0)
        < lax.broadcasted_iota(jnp.int32, (row_count, row_count), 1),
        1.0,
        0.0,
    )
    earlier = jnp.dot(
        routed.astype(jnp.bfloat16), before.astype(jnp.bfloat16), preferred_element_type=jnp.float32
    )
    place = (slot - expert_of * cap).astype(jnp.float32)
    chosen = jnp.where(earlier == place, routed, 0.0)
    weighted = chosen * share

    q_rows[...] = jnp.zeros_like(q_rows)
    loads[0].wait()
    for kv in range(kv_local):
        for g in range(group):
            head = kv * group + g
            q_rows[pl.ds(kv * SLOTS + g, row_count, stride=stride), :] = q_buf[
                :, head * HEAD : (head + 1) * HEAD
            ].astype(jnp.float32)
    loads[1].wait()
    loads[2].wait()
    key_head = lax.broadcasted_iota(jnp.int32, (stride, HEAD), 0) // SLOTS
    position = lax.broadcasted_iota(jnp.int32, (stride, context), 1)
    block = 8

    def attend(blk, carry):
        for i in range(block):
            r = blk * block + i
            start = pl.multiple_of(r * stride, stride)
            q = q_rows[pl.ds(start, stride), :]
            q = jnp.concatenate(
                [jnp.where(key_head == kv, q, 0.0) for kv in range(kv_local)], axis=1
            ).astype(jnp.bfloat16)
            scores = lax.dot_general(
                q, k_buf[r], (((1,), (1,)), ((), ())), preferred_element_type=jnp.float32
            ) / math.sqrt(HEAD)
            scores = jnp.where(position < lengths[r], scores, -jnp.inf)
            scaled = jnp.exp(scores - jnp.max(scores, axis=-1, keepdims=True))
            prob = (scaled / jnp.sum(scaled, axis=-1, keepdims=True)).astype(jnp.bfloat16)
            att = jnp.dot(prob, v_buf[r], preferred_element_type=jnp.float32)
            for kv in range(kv_local):
                att_rows[pl.ds(start + kv * SLOTS, SLOTS), :] = att[
                    kv * SLOTS : (kv + 1) * SLOTS, kv * HEAD : (kv + 1) * HEAD
                ]
        return carry

    lax.fori_loop(0, row_count // block, attend, 0)
    loads[3].wait()
    for kv in range(kv_local):
        for g in range(group):
            columns = slice((kv * group + g) * HEAD, (kv * group + g + 1) * HEAD)
            hidden[:, columns] = (
                res_buf[:, columns].astype(jnp.float32)
                + att_rows[pl.ds(kv * SLOTS + g, row_count, stride=stride), :]
            )

    picked = jnp.dot(
        chosen.astype(jnp.bfloat16),
        hidden[...].astype(jnp.bfloat16),
        preferred_element_type=jnp.float32,
    )
    for e in range(EXPERTS):
        rows = picked[e * cap : (e + 1) * cap]
        outgoing[e] = jnp.concatenate([rows[:, :half], rows[:, half:]], axis=0).astype(jnp.bfloat16)
    arrived[c, b] = outgoing[b // splits]

    pl.semaphore_wait(barrier, devices - 1 + cuts - 1)

    def row_copy(to):
        return pltpu.make_async_remote_copy(
            src_ref=outgoing.at[to // splits],
            dst_ref=arrived.at[c, b],
            send_sem=row_send.at[to],
            recv_sem=row_recv.at[b],
            device_id={"expert": to},
            device_id_type=MESH,
        )

    each(1, devices, lambda i: row_copy(lax.rem(b + i, devices)).start())

    def forward(a):
        for peer in order[:0:-1]:
            pltpu.make_async_remote_copy(
                src_ref=arrived.at[c, a],
                dst_ref=arrived.at[c, a],
                send_sem=share_send.at[peer],
                recv_sem=share_recv.at[c],
                device_id={"cuts": peer},
                device_id_type=MESH,
            ).start()

    forward(b)

    def take(i):
        a = lax.rem(b + devices - i, devices)
        pltpu.make_async_remote_copy(
            src_ref=arrived.at[c, a],
            dst_ref=arrived.at[c, a],
            send_sem=row_send.at[a],
            recv_sem=row_recv.at[a],
            device_id={"expert": a},
            device_id_type=MESH,
        ).wait_recv()
        forward(a)

    each(1, devices, take)

    def whole_share(peer):
        return pltpu.make_async_remote_copy(
            src_ref=arrived.at[peer],
            dst_ref=arrived.at[peer],
            send_sem=share_send.at[peer],
            recv_sem=share_recv.at[peer],
            device_id={"cuts": peer},
            device_id_type=MESH,
        )

    tile = 512 if ff % 512 == 0 else ff
    for i in range(cuts):
        if i:
            whole_share(order[i]).wait_recv()

        def pack(pair, i=i):
            first = arrived[order[i], 2 * pair].astype(jnp.float32)
            second = arrived[order[i], 2 * pair + 1].astype(jnp.float32)
            rows = pl.ds(pair * 2 * cap, 2 * cap)
            stacked[rows, :half] = jnp.concatenate([first[:cap], second[:cap]], axis=0).astype(
                jnp.bfloat16
            )
            stacked[rows, half:] = jnp.concatenate([first[cap:], second[cap:]], axis=0).astype(
                jnp.bfloat16
            )

        each(0, devices // 2, pack)
        gate_loads[i].wait()
        up_loads[i].wait()

        def project(n, carry, i=i):
            columns = pl.ds(pl.multiple_of(n * tile, tile), tile)
            x = stacked[...]
            for weight, total in ((wg, gate_act), (wu, up_act)):
                part = jnp.dot(x, weight[i, :, columns], preferred_element_type=jnp.float32)
                total[:, columns] = part if i == 0 else total[:, columns] + part
            return carry

        lax.fori_loop(0, ff // tile, project, 0)

    gated = gate_act[...]
    act[...] = (gated / (1.0 + jnp.exp(-gated)) * up_act[...]).astype(jnp.bfloat16)

    def sum_copy(j):
        peer = order[cuts - 1 - j]
        return pltpu.make_async_remote_copy(
            src_ref=cut_send.at[j],
            dst_ref=cut_recv.at[c],
            send_sem=sum_send.at[j],
            recv_sem=sum_recv.at[c],
            device_id={"cuts": peer},
            device_id_type=MESH,
        )

    out_tile = half if half % 128 == 0 else width
    for j in range(cuts):
        down_loads[j].wait()

        def expand(n, carry, j=j):
            columns = pl.ds(pl.multiple_of(n * out_tile, out_tile), out_tile)
            part = jnp.dot(act[...], wd[j, :, columns], preferred_element_type=jnp.float32)
            if j < cuts - 1:
                cut_send[j, :, columns] = part.astype(jnp.bfloat16)
            else:
                own[:, columns] = part
            return carry

        lax.fori_loop(0, width // out_tile, expand, 0)
        if j < cuts - 1:
            sum_copy(j).start()

    for peer in order[1:]:
        pltpu.make_async_remote_copy(
            src_ref=cut_recv.at[peer],
            dst_ref=cut_recv.at[peer],
            send_sem=sum_send.at[0],
            recv_sem=sum_recv.at[peer],
            device_id={"cuts": peer},
            device_id_type=MESH,
        ).wait_recv()

    def total(pair):
        rows = pl.ds(pair * 2 * cap, 2 * cap)
        value = own[rows, :]
        for peer in order[1:]:
            value = value + cut_recv[peer, rows, :].astype(jnp.float32)
        for k in range(2):
            mine = value[k * cap : (k + 1) * cap]
            back_send[2 * pair + k] = jnp.concatenate(
                [mine[:, :half], mine[:, half:]], axis=0
            ).astype(jnp.bfloat16)

    each(0, devices // 2, total)

    def back_copy(to):
        return pltpu.make_async_remote_copy(
            src_ref=back_send.at[to],
            dst_ref=back_recv.at[b],
            send_sem=ret_send.at[to],
            recv_sem=ret_recv.at[b],
            device_id={"expert": to},
            device_id_type=MESH,
        )

    each(1, devices, lambda i: back_copy(lax.rem(b + i, devices)).start())
    back_recv[b] = back_send[b]

    each(1, devices, lambda i: row_copy(lax.rem(b + i, devices)).wait_send())
    for peer in order[1:]:
        whole_share(peer).wait_send()
    for j in range(cuts - 1):
        sum_copy(j).wait_send()

    def returned(i):
        a = lax.rem(b + devices - i, devices)
        pltpu.make_async_remote_copy(
            src_ref=back_recv.at[a],
            dst_ref=back_recv.at[a],
            send_sem=ret_send.at[a],
            recv_sem=ret_recv.at[a],
            device_id={"expert": a},
            device_id_type=MESH,
        ).wait_recv()

    each(1, devices, returned)
    sums = []
    for e in range(EXPERTS):
        value = back_recv[e * splits].astype(jnp.float32)
        for s in range(1, splits):
            value = value + back_recv[e * splits + s].astype(jnp.float32)
        sums.append(value)
    for h in range(2):
        columns = slice(h * half, (h + 1) * half)
        stack = jnp.concatenate([value[h * cap : (h + 1) * cap] for value in sums], axis=0)
        combined = lax.dot_general(
            weighted,
            stack,
            (((0,), (0,)), ((), ())),
            preferred_element_type=jnp.float32,
            precision=lax.Precision.HIGHEST,
        )
        out[:, columns] = (hidden[:, columns] + combined).astype(jnp.bfloat16)
    each(1, devices, lambda i: back_copy(lax.rem(b + i, devices)).wait_send())


def on_device(
    devices,
    cuts,
    queries,
    key_cache,
    value_cache,
    lengths,
    residual,
    routes,
    route_weight,
    gate_weight,
    up_weight,
    down_weight,
):
    row_count, width = queries.shape
    cap = (row_count * TOPK + MODEL_EXPERTS - 1) // MODEL_EXPERTS
    ff = gate_weight.shape[2]
    kv_width = key_cache.shape[2]
    stride = kv_width // HEAD * SLOTS
    items = devices * cap
    bf16, f32 = jnp.bfloat16, jnp.float32
    dma = pltpu.SemaphoreType.DMA
    vmem = pl.BlockSpec(memory_space=pltpu.VMEM)
    anywhere = pl.BlockSpec(memory_space=pl.ANY)
    return pl.pallas_call(
        functools.partial(kernel, devices, cuts, cap),
        out_shape=jax.ShapeDtypeStruct((row_count, width), bf16),
        in_specs=[pl.BlockSpec(memory_space=pltpu.SMEM), vmem, vmem] + [anywhere] * 7,
        out_specs=vmem,
        scratch_shapes=[
            pltpu.VMEM((row_count, width), bf16),
            pltpu.VMEM(key_cache.shape, bf16),
            pltpu.VMEM(value_cache.shape, bf16),
            pltpu.VMEM((row_count, width), bf16),
            pltpu.VMEM((row_count * stride, HEAD), f32),
            pltpu.VMEM((row_count * stride, HEAD), f32),
            pltpu.VMEM((row_count, width), f32),
            pltpu.VMEM((cuts, width, ff), bf16),
            pltpu.VMEM((cuts, width, ff), bf16),
            pltpu.VMEM((cuts, ff, width), bf16),
            pltpu.VMEM((EXPERTS, 2 * cap, width // 2), bf16),
            pltpu.VMEM((cuts, devices, 2 * cap, width // 2), bf16),
            pltpu.VMEM((items, width), bf16),
            pltpu.VMEM((items, ff), f32),
            pltpu.VMEM((items, ff), f32),
            pltpu.VMEM((items, ff), bf16),
            pltpu.VMEM((cuts - 1, items, width), bf16),
            pltpu.VMEM((cuts, items, width), bf16),
            pltpu.VMEM((items, width), f32),
            pltpu.VMEM((devices, 2 * cap, width // 2), bf16),
            pltpu.VMEM((devices, 2 * cap, width // 2), bf16),
            dma((4,)),
            dma((cuts,)),
            dma((cuts,)),
            dma((cuts,)),
            dma((devices,)),
            dma((devices,)),
            dma((cuts,)),
            dma((cuts,)),
            dma((cuts - 1,)),
            dma((cuts,)),
            dma((devices,)),
            dma((devices,)),
        ],
        compiler_params=pltpu.CompilerParams(
            collective_id=0, has_side_effects=True, vmem_limit_bytes=60 * 1024 * 1024
        ),
    )(
        lengths,
        routes.T,
        route_weight.T,
        queries,
        key_cache,
        value_cache,
        residual,
        gate_weight,
        up_weight,
        down_weight,
    )


def solution(mesh):
    return jax.shard_map(
        functools.partial(on_device, mesh.shape["expert"], mesh.shape["cuts"]),
        mesh=mesh,
        in_specs=(
            P(("groups", "expert"), "cuts"),
            P(("groups", "expert"), None, "cuts"),
            P(("groups", "expert"), None, "cuts"),
            P(("groups", "expert")),
            P(("groups", "expert"), "cuts"),
            P(("groups", "expert"), None),
            P(("groups", "expert"), None),
            P("expert", None, "cuts"),
            P("expert", None, "cuts"),
            P("expert", "cuts", None),
        ),
        out_specs=P(("groups", "expert"), "cuts"),
        check_vma=False,
    )
```

time: 106 us -> 44.5 us (0.42)
  Pallas kernels: 0 us -> 42.8 us
  waiting for transfers between devices: 40.6 us -> 0 us
  matrix products: 25.2 us -> 0 us
  blocking collectives: 18.4 us -> 0 us
  between operations: 13.5 us -> 0.01 us
  starting transfers between devices: 3.53 us -> 0 us
  other arithmetic: 3.48 us -> 0 us
    pallas_call x0 -> x1, Pallas kernels: none -> 42.8 us  [on_device(): pl.pallas_call(functools.partial(kernel, devices, cuts, cap), out_shape=j...]
    dot_general x6 -> x0, matrix products: 25.2 us -> none  [the longest x1 13.4 us: on_device(): jnp.dot(activated, down_weight[0], preferred_element_type=jnp.float32)]
    all_to_all x1 -> x0, waiting for transfers between devices: 20.8 us -> none  [on_device(): lax.all_to_all(partial_out, 'expert', split_axis=0, concat_axis=0, tiled=...]
    reduce_scatter x1 -> x0, waiting for transfers between devices: 19.8 us -> none  [on_device(): lax.psum_scatter(full_rows.astype(jnp.bfloat16), 'cuts', scatter_dimensio...]
    all_to_all x1 -> x0, blocking collectives: 12 us -> none  [on_device(): lax.all_to_all(outgoing, 'expert', split_axis=0, concat_axis=0, tiled=True)]
    all_gather x1 -> x0, blocking collectives: 6.44 us -> none  [on_device(): lax.all_gather(lax.all_to_all(outgoing, 'expert', split_axis=0, concat_ax...]
    all_to_all x1 -> x0, starting transfers between devices: 3.49 us -> none  [on_device(): lax.all_to_all(partial_out, 'expert', split_axis=0, concat_axis=0, tiled=...]
    convert_element_type x1 -> x0, other arithmetic: 1.56 us -> none  [on_device(): return (hidden + combined).astype(jnp.bfloat16)]
  transfers between devices with their start and end apart: 2 -> 0, of which waited for: 2 -> 0; matrix products, arithmetic and copies ran while one was open for 0% -> 0% of each run, Pallas kernels for 0% -> 0%
where the time goes in v1:
time: 44.5 us; the launch traced here: 44.3 us
  Pallas kernels  42.8 us (96%)
  local copies, waits for them, and re-layouts  1.54 us (3%)
    pallas_call x1, Pallas kernels, on_device(): pl.pallas_call(functools.partial(kernel, devices, cuts, cap), out_shape=j...  42.8 us
    unnamed x1, local copies, waits for them, and re-layouts  1.54 us

profile of v1, /device:TPU:0, one launch (start us, length us, event | category | flops | bytes accessed | tf_op | source)
XLA Modules:
  0.0 44.3 jit_solution(9364204023964709566)
XLA Ops:
  0.0 42.8 %shard_map.100 = bf16[32,1536]{1,0:T(8,128)(2,1)} custom-call(s32[32]{0:T(128)} %lengths.1, s32[4,32]{1,0:T(4,128)} %bitcast.2, f32[4,32]{1,0:T(4,128)} %bitcast.3, bf16[32,1536]{1,0:T(8,128)(2,1)} %queries.1, bf16[32,96,256]{2,1,0:T(8,128)(2,1)} %keys.1, bf16[32,96,256]{2,1,0:T(8,128)(2,1)} %values.1, bf16[32,1536]{1,0:T(8,128)(2,1)} %residual.1, ...), custom_call_target="tpu_custom_call" | custom-call | tf_op jit(solution)/shard_map/pallas_call | solution.py:421
  42.8 1.5 %copy.12 = bf16[32,1536]{1,0:T(8,128)(2,1)} copy(bf16[32,1536]{1,0:T(8,128)(2,1)} %shard_map.100) | data formatting | bytes 196608

commit v2 on v1

--- a/solution.py
+++ b/solution.py
@@ -126,11 +126,6 @@
         down_loads.append(pltpu.make_async_copy(down.at[0, :, columns], wd.at[i], wd_sem.at[i]))
     for load in loads:
         load.start()
-    for g, u in zip(gate_loads, up_loads):
-        g.start()
-        u.start()
-    for d in down_loads:
-        d.start()
 
     slot = lax.broadcasted_iota(jnp.int32, (EXPERTS * cap, row_count), 0)
     expert_of = slot // cap
@@ -163,25 +158,42 @@
             ].astype(jnp.float32)
     loads[1].wait()
     loads[2].wait()
+    for g, u in zip(gate_loads, up_loads):
+        g.start()
+        u.start()
+    for d in down_loads:
+        d.start()
     key_head = lax.broadcasted_iota(jnp.int32, (stride, HEAD), 0) // SLOTS
     position = lax.broadcasted_iota(jnp.int32, (stride, context), 1)
-    block = 8
+    block = min(16, row_count)
 
     def attend(blk, carry):
-        for i in range(block):
-            r = blk * block + i
-            start = pl.multiple_of(r * stride, stride)
+        rows = [blk * block + i for i in range(block)]
+        starts = [pl.multiple_of(r * stride, stride) for r in rows]
+        scores, probs = [], []
+        for r, start in zip(rows, starts):
             q = q_rows[pl.ds(start, stride), :]
             q = jnp.concatenate(
                 [jnp.where(key_head == kv, q, 0.0) for kv in range(kv_local)], axis=1
             ).astype(jnp.bfloat16)
-            scores = lax.dot_general(
-                q, k_buf[r], (((1,), (1,)), ((), ())), preferred_element_type=jnp.float32
-            ) / math.sqrt(HEAD)
-            scores = jnp.where(position < lengths[r], scores, -jnp.inf)
-            scaled = jnp.exp(scores - jnp.max(scores, axis=-1, keepdims=True))
-            prob = (scaled / jnp.sum(scaled, axis=-1, keepdims=True)).astype(jnp.bfloat16)
-            att = jnp.dot(prob, v_buf[r], preferred_element_type=jnp.float32)
+            scores.append(
+                lax.dot_general(
+                    q, k_buf[r], (((1,), (1,)), ((), ())), preferred_element_type=jnp.float32
+                )
+            )
+        scores = [
+            jnp.where(position < lengths[r], score / math.sqrt(HEAD), -jnp.inf)
+            for r, score in zip(rows, scores)
+        ]
+        highest = [jnp.max(score, axis=-1, keepdims=True) for score in scores]
+        scaled = [jnp.exp(score - high) for score, high in zip(scores, highest)]
+        sums = [jnp.sum(value, axis=-1, keepdims=True) for value in scaled]
+        probs = [(value / part).astype(jnp.bfloat16) for value, part in zip(scaled, sums)]
+        atts = [
+            jnp.dot(prob, v_buf[r], preferred_element_type=jnp.float32)
+            for r, prob in zip(rows, probs)
+        ]
+        for start, att in zip(starts, atts):
             for kv in range(kv_local):
                 att_rows[pl.ds(start + kv * SLOTS, SLOTS), :] = att[
                     kv * SLOTS : (kv + 1) * SLOTS, kv * HEAD : (kv + 1) * HEAD

time: 44.5 us -> 32.2 us (0.72)
  Pallas kernels: 42.8 us -> 30.5 us
    pallas_call x1, Pallas kernels: 42.8 us -> 30.5 us  [on_device(): pl.pallas_call(functools.partial(kernel, devices, cuts, cap), out_shape=j...]
where the time goes in v2:
time: 32.2 us; the launch traced here: 32 us
  Pallas kernels  30.5 us (95%)
  local copies, waits for them, and re-layouts  1.54 us (5%)
    pallas_call x1, Pallas kernels, on_device(): pl.pallas_call(functools.partial(kernel, devices, cuts, cap), out_shape=j...  30.5 us
    unnamed x1, local copies, waits for them, and re-layouts  1.54 us

profile of v2, /device:TPU:0, one launch (start us, length us, event | category | flops | bytes accessed | tf_op | source)
XLA Modules:
  0.0 32.0 jit_solution(2473405815287613735)
XLA Ops:
  0.0 30.5 %shard_map.100 = bf16[32,1536]{1,0:T(8,128)(2,1)} custom-call(s32[32]{0:T(128)} %lengths.1, s32[4,32]{1,0:T(4,128)} %bitcast.2, f32[4,32]{1,0:T(4,128)} %bitcast.3, bf16[32,1536]{1,0:T(8,128)(2,1)} %queries.1, bf16[32,96,256]{2,1,0:T(8,128)(2,1)} %keys.1, bf16[32,96,256]{2,1,0:T(8,128)(2,1)} %values.1, bf16[32,1536]{1,0:T(8,128)(2,1)} %residual.1, ...), custom_call_target="tpu_custom_call" | custom-call | tf_op jit(solution)/shard_map/pallas_call | solution.py:433
  30.5 1.5 %copy.12 = bf16[32,1536]{1,0:T(8,128)(2,1)} copy(bf16[32,1536]{1,0:T(8,128)(2,1)} %shard_map.100) | data formatting | bytes 196608

commit v3 on v2

--- a/solution.py
+++ b/solution.py
@@ -72,6 +72,7 @@
     cut_send,
     cut_recv,
     own,
+    paired,
     back_send,
     back_recv,
     in_sem,
@@ -161,8 +162,6 @@
     for g, u in zip(gate_loads, up_loads):
         g.start()
         u.start()
-    for d in down_loads:
-        d.start()
     key_head = lax.broadcasted_iota(jnp.int32, (stride, HEAD), 0) // SLOTS
     position = lax.broadcasted_iota(jnp.int32, (stride, context), 1)
     block = min(16, row_count)
@@ -246,6 +245,8 @@
             ).start()
 
     forward(b)
+    for d in down_loads:
+        d.start()
 
     def take(i):
         a = lax.rem(b + devices - i, devices)
@@ -305,34 +306,17 @@
     act[...] = (gated / (1.0 + jnp.exp(-gated)) * up_act[...]).astype(jnp.bfloat16)
 
     def sum_copy(j):
-        peer = order[cuts - 1 - j]
+        peer = order[1] if cuts == 4 and j == 0 else order[cuts - 1 - j]
         return pltpu.make_async_remote_copy(
             src_ref=cut_send.at[j],
-            dst_ref=cut_recv.at[c],
+            dst_ref=cut_recv.at[order[2] if cuts == 4 and j == 0 else c],
             send_sem=sum_send.at[j],
-            recv_sem=sum_recv.at[c],
+            recv_sem=sum_recv.at[order[2] if cuts == 4 and j == 0 else c],
             device_id={"cuts": peer},
             device_id_type=MESH,
         )
 
-    out_tile = half if half % 128 == 0 else width
-    for j in range(cuts):
-        down_loads[j].wait()
-
-        def expand(n, carry, j=j):
-            columns = pl.ds(pl.multiple_of(n * out_tile, out_tile), out_tile)
-            part = jnp.dot(act[...], wd[j, :, columns], preferred_element_type=jnp.float32)
-            if j < cuts - 1:
-                cut_send[j, :, columns] = part.astype(jnp.bfloat16)
-            else:
-                own[:, columns] = part
-            return carry
-
-        lax.fori_loop(0, width // out_tile, expand, 0)
-        if j < cuts - 1:
-            sum_copy(j).start()
-
-    for peer in order[1:]:
+    def sum_arrived(peer):
         pltpu.make_async_remote_copy(
             src_ref=cut_recv.at[peer],
             dst_ref=cut_recv.at[peer],
@@ -342,10 +326,45 @@
             device_id_type=MESH,
         ).wait_recv()
 
+    out_tile = half if half % 128 == 0 else width
+    for j in range(cuts):
+        down_loads[j].wait()
+
+        def expand(n, carry, j=j):
+            columns = pl.ds(pl.multiple_of(n * out_tile, out_tile), out_tile)
+            part = jnp.dot(act[...], wd[j, :, columns], preferred_element_type=jnp.float32)
+            if cuts == 4 and j == 1:
+                paired[:, columns] = part
+            elif j < cuts - 1:
+                cut_send[j, :, columns] = part.astype(jnp.bfloat16)
+            else:
+                own[:, columns] = part
+            return carry
+
+        lax.fori_loop(0, width // out_tile, expand, 0)
+        if cuts == 4 and j == 2:
+            sum_copy(2).start()
+            sum_arrived(order[3])
+            items = paired.shape[0]
+
+            def pair_sum(n):
+                rows = pl.ds(n * 2 * cap, 2 * cap)
+                both = paired[rows, :] + cut_recv[order[3], rows, :].astype(jnp.float32)
+                cut_send[1, rows, :] = both.astype(jnp.bfloat16)
+
+            each(0, items // (2 * cap), pair_sum)
+            sum_copy(1).start()
+        elif j < cuts - 1 and not (cuts == 4 and j == 1):
+            sum_copy(j).start()
+
+    senders = [order[1], order[2]] if cuts == 4 else order[1:]
+    for peer in senders:
+        sum_arrived(peer)
+
     def total(pair):
         rows = pl.ds(pair * 2 * cap, 2 * cap)
         value = own[rows, :]
-        for peer in order[1:]:
+        for peer in senders:
             value = value + cut_recv[peer, rows, :].astype(jnp.float32)
         for k in range(2):
             mine = value[k * cap : (k + 1) * cap]
@@ -455,6 +474,7 @@
             pltpu.VMEM((cuts - 1, items, width), bf16),
             pltpu.VMEM((cuts, items, width), bf16),
             pltpu.VMEM((items, width), f32),
+            pltpu.VMEM((items, width), f32),
             pltpu.VMEM((devices, 2 * cap, width // 2), bf16),
             pltpu.VMEM((devices, 2 * cap, width // 2), bf16),
             dma((4,)),

time: 32.2 us -> 29.6 us (0.919)
  Pallas kernels: 30.5 us -> 27.9 us
    pallas_call x1, Pallas kernels: 30.5 us -> 27.9 us  [on_device(): pl.pallas_call(functools.partial(kernel, devices, cuts, cap), out_shape=j...]
where the time goes in v3:
time: 29.6 us; the launch traced here: 29.5 us
  Pallas kernels  27.9 us (94%)
  local copies, waits for them, and re-layouts  1.54 us (5%)
    pallas_call x1, Pallas kernels, on_device(): pl.pallas_call(functools.partial(kernel, devices, cuts, cap), out_shape=j...  27.9 us
    unnamed x1, local copies, waits for them, and re-layouts  1.54 us

profile of v3, /device:TPU:0, one launch (start us, length us, event | category | flops | bytes accessed | tf_op | source)
XLA Modules:
  0.0 29.5 jit_solution(8462667414386404810)
XLA Ops:
  0.0 27.9 %shard_map.100 = bf16[32,1536]{1,0:T(8,128)(2,1)} custom-call(s32[32]{0:T(128)} %lengths.1, s32[4,32]{1,0:T(4,128)} %bitcast.2, f32[4,32]{1,0:T(4,128)} %bitcast.3, bf16[32,1536]{1,0:T(8,128)(2,1)} %queries.1, bf16[32,96,256]{2,1,0:T(8,128)(2,1)} %keys.1, bf16[32,96,256]{2,1,0:T(8,128)(2,1)} %values.1, bf16[32,1536]{1,0:T(8,128)(2,1)} %residual.1, ...), custom_call_target="tpu_custom_call" | custom-call | tf_op jit(solution)/shard_map/pallas_call | solution.py:452
  27.9 1.5 %copy.12 = bf16[32,1536]{1,0:T(8,128)(2,1)} copy(bf16[32,1536]{1,0:T(8,128)(2,1)} %shard_map.100) | data formatting | bytes 196608

commit v4 on v3

--- a/solution.py
+++ b/solution.py
@@ -233,8 +233,10 @@
 
     each(1, devices, lambda i: row_copy(lax.rem(b + i, devices)).start())
 
+    nearest = [order[2], order[1]] if cuts == 4 else order[1:]
+
     def forward(a):
-        for peer in order[:0:-1]:
+        for peer in nearest:
             pltpu.make_async_remote_copy(
                 src_ref=arrived.at[c, a],
                 dst_ref=arrived.at[c, a],
@@ -272,9 +274,22 @@
             device_id_type=MESH,
         )
 
+    def relay():
+        return pltpu.make_async_remote_copy(
+            src_ref=arrived.at[order[2]],
+            dst_ref=arrived.at[order[2]],
+            send_sem=share_send.at[c],
+            recv_sem=share_recv.at[order[2]],
+            device_id={"cuts": order[1]},
+            device_id_type=MESH,
+        )
+
     tile = 512 if ff % 512 == 0 else ff
     for i in range(cuts):
-        if i:
+        if cuts == 4 and i == 1:
+            whole_share(order[2]).wait_recv()
+            relay().start()
+        if i and not (cuts == 4 and i == 2):
             whole_share(order[i]).wait_recv()
 
         def pack(pair, i=i):
@@ -388,8 +403,10 @@
     back_recv[b] = back_send[b]
 
     each(1, devices, lambda i: row_copy(lax.rem(b + i, devices)).wait_send())
-    for peer in order[1:]:
+    for peer in nearest:
         whole_share(peer).wait_send()
+    if cuts == 4:
+        relay().wait_send()
     for j in range(cuts - 1):
         sum_copy(j).wait_send()
 

time: 29.6 us -> 30.5 us (1.030)
  Pallas kernels: 27.9 us -> 28.7 us
    pallas_call x1, Pallas kernels: 27.9 us -> 28.7 us  [on_device(): pl.pallas_call(functools.partial(kernel, devices, cuts, cap), out_shape=j...]
where the time goes in v4:
time: 30.5 us; the launch traced here: 30.3 us
  Pallas kernels  28.7 us (94%)
  local copies, waits for them, and re-layouts  1.54 us (5%)
    pallas_call x1, Pallas kernels, on_device(): pl.pallas_call(functools.partial(kernel, devices, cuts, cap), out_shape=j...  28.7 us
    unnamed x1, local copies, waits for them, and re-layouts  1.54 us

profile of v4, /device:TPU:0, one launch (start us, length us, event | category | flops | bytes accessed | tf_op | source)
XLA Modules:
  0.0 30.3 jit_solution(15037513300393818416)
XLA Ops:
  0.0 28.7 %shard_map.100 = bf16[32,1536]{1,0:T(8,128)(2,1)} custom-call(s32[32]{0:T(128)} %lengths.1, s32[4,32]{1,0:T(4,128)} %bitcast.2, f32[4,32]{1,0:T(4,128)} %bitcast.3, bf16[32,1536]{1,0:T(8,128)(2,1)} %queries.1, bf16[32,96,256]{2,1,0:T(8,128)(2,1)} %keys.1, bf16[32,96,256]{2,1,0:T(8,128)(2,1)} %values.1, bf16[32,1536]{1,0:T(8,128)(2,1)} %residual.1, ...), custom_call_target="tpu_custom_call" | custom-call | tf_op jit(solution)/shard_map/pallas_call | solution.py:469
  28.7 1.5 %copy.12 = bf16[32,1536]{1,0:T(8,128)(2,1)} copy(bf16[32,1536]{1,0:T(8,128)(2,1)} %shard_map.100) | data formatting | bytes 196608
